TPU v7x, 32 devices: a whole 2x2x4 slice. The times are simulated.
32 devices in a mesh: layer: 4 (over x, core), rows: 8 (over z, y).
Axes of the slice: x: 2, y: 2, z: 4, core: 2. Of those that a mesh axis runs over, the one named last changes fastest.
Arguments:
- key_weight: bfloat16 [4, 8192, 512], P('layer', 'rows'), may hold values from -0.0625 to 0.0625
- value_weight: bfloat16 [4, 8192, 512], P('layer', 'rows'), may hold values from -0.0625 to 0.0625
- key_grad: bfloat16 [4, 8192, 512], P('layer', 'rows'), may hold values from -8000 to 8000
- value_grad: bfloat16 [4, 8192, 512], P('layer', 'rows'), may hold values from -8000 to 8000
Outputs:
- key_update: bfloat16 [4, 8192, 512], P('layer', 'rows')
- value_update: bfloat16 [4, 8192, 512], P('layer', 'rows')
- key_dual: float32 [4, 512, 512], P('layer', 'rows')
- value_dual: float32 [4, 512, 512], P('layer', 'rows')
All inputs are finite; a program needn't handle non-finite values.
Results may differ from a plain program's by a relative error of at most 0.033.
Values may be sent and summed in bfloat16 or wider, within the bound.
A program may use at most 64 MiB of HBM per device.

v0:
```python
import jax
import jax.numpy as jnp
from jax import lax
from jax.sharding import PartitionSpec as P

DUAL_ITERS = 2
NS_STEPS = 3


first_coeff = 3.4445
third_coeff = -4.775
fifth_coeff = 2.0315
learn_rate = 0.1
dual_rate = 4.0
clip_target = 0.02
epsilon = 1e-06
highest = lax.Precision.HIGHEST


def products(left, right):
    return jnp.einsum("brc,brd->bcd", left, right, preferred_element_type=jnp.float32)


def apply_right(left, right):
    return jnp.einsum("brc,bcd->brd", left, right, preferred_element_type=jnp.float32)


def polynomial(partial_value, squares, first):
    summed = lax.psum(partial_value.astype(jnp.bfloat16), "rows").astype(jnp.float32)
    if first:
        summed = summed / (squares + epsilon)[:, None, None]
    quartic = jnp.einsum("bcd,bde->bce", summed, summed, precision=highest)
    result = (third_coeff * summed + fifth_coeff * quartic).astype(jnp.bfloat16)
    return (result, squares)


def orthogonalize(shifted):
    squares = None
    squares = lax.psum(jnp.sum(jnp.square(shifted.astype(jnp.float32)), axis=(1, 2)), "rows")
    poly, squares = polynomial(products(shifted, shifted), squares, True)
    inverse = lax.rsqrt(squares + epsilon)[:, None, None]
    iterate = (
        (first_coeff * shifted.astype(jnp.float32) + apply_right(shifted, poly)) * inverse
    ).astype(jnp.bfloat16)
    for repeat in range(NS_STEPS - 1):
        poly, unused = polynomial(products(iterate, iterate), None, False)
        iterate = (first_coeff * iterate.astype(jnp.float32) + apply_right(iterate, poly)).astype(
            jnp.bfloat16
        )
    return iterate


def on_device(key_weight, value_weight, key_grad, value_grad):
    layer_count = key_weight.shape[0]
    weights = jnp.concatenate([key_weight, value_weight], 0)
    grads = jnp.concatenate([key_grad, value_grad], 0)
    local_sum = jnp.sum(jnp.square(grads.astype(jnp.float32)))
    total = lax.psum(local_sum, ("layer", "rows"))
    entries = float(grads.size * lax.axis_size("layer") * lax.axis_size("rows"))
    clip = clip_target / jnp.sqrt(total / entries + epsilon)
    dual = None
    iterate = weights
    for iteration in range(DUAL_ITERS):
        if dual is None:
            shifted = (clip * grads.astype(jnp.float32)).astype(jnp.bfloat16)
        else:
            shift_rows = (4.0 * dual).astype(jnp.bfloat16)
            shift = lax.all_gather(shift_rows, "rows", axis=1, tiled=True)
            shifted = (clip * grads.astype(jnp.float32) + apply_right(weights, shift)).astype(
                jnp.bfloat16
            )
        iterate = orthogonalize(shifted)
        cross = products(weights, iterate)
        term = dual_rate * -learn_rate * (cross + jnp.swapaxes(cross, 1, 2))
        step_rows = lax.psum_scatter(
            term.astype(jnp.bfloat16), "rows", scatter_dimension=1, tiled=True
        ).astype(jnp.float32)
        dual = step_rows if dual is None else dual + step_rows
    update = (-learn_rate * iterate.astype(jnp.float32)).astype(jnp.bfloat16)
    return (update[:layer_count], update[layer_count:], dual[:layer_count], dual[layer_count:])


def solution(mesh):
    placed = (
        P("layer", "rows", None),
        P("layer", "rows", None),
        P("layer", "rows", None),
        P("layer", "rows", None),
    )
    return jax.shard_map(
        on_device,
        mesh=mesh,
        in_specs=placed,
        out_specs=(
            P("layer", "rows", None),
            P("layer", "rows", None),
            P("layer", "rows", None),
            P("layer", "rows", None),
        ),
        check_vma=False,
    )
```

profile of v0, /device:TPU:0, one launch (start us, length us, event | category | flops | bytes accessed | tf_op | source)
XLA Modules:
  0.0 770.0 jit_solution(7711575444790275356)
XLA Ops:
  7.2 3.4 fusion.3
  10.6 42.2 %psum.63 = f32[]{:T(128)} all-reduce(f32[]{:T(128)} %fusion.3), channel_id=1, replica_groups=mesh['layer'=4,'rows'=8] {'layer','rows'}, use_global_device_ids=true, to_apply=%region_1.0 | all-reduce | flops 1 | bytes 8 | tf_op jit(solution)/shard_map/psum | solution.py:58
  53.5 2.3 fusion.19
  55.9 0.7 fusion.7
  56.5 21.3 %psum.65 = f32[2]{0:T(128)S(1)} all-reduce(f32[2]{0:T(128)S(1)} %fusion.7), channel_id=1, replica_groups=mesh['layer'=4,'rows'=8] {'rows'}, use_global_device_ids=true, to_apply=%region_4.0 | all-reduce | flops 2 | bytes 16 | tf_op jit(solution)/shard_map/psum | solution.py:39
  77.9 56.5 %all-reduce.7.cloned.1.call-done = bf16[2,512,512]{2,1,0:T(8,128)(2,1)} async-done(((bf16[2,512,512]{2,1,0:T(8,128)(2,1)}), bf16[2,512,512]{2,1,0:T(8,128)(2,1)}) %all-reduce.7.cloned.1.call-update) | async-done | bytes 1048592 | tf_op jit(solution)/shard_map/psum | solution.py:29
  134.3 6.0 add_convert_fusion.9
  140.4 1.6 fusion.6
  142.0 1.3 copy-done.9
  143.3 2.3 convolution_convert_fusion.4
  145.8 77.7 %all-reduce.9.cloned.1.call-done = bf16[2,512,512]{2,1,0:T(8,128)(2,1)} async-done(((bf16[2,512,512]{2,1,0:T(8,128)(2,1)}), bf16[2,512,512]{2,1,0:T(8,128)(2,1)}) %all-reduce.9.cloned.1.call-update) | async-done | bytes 1048592 | tf_op jit(solution)/shard_map/psum | solution.py:29
  223.5 2.8 add_convert_fusion.8
  226.4 1.3 add_convert_fusion.3
  227.6 1.3 copy-done.7
  229.0 2.3 convolution_convert_fusion.3
  231.3 1.3 copy.8
  232.7 1.3 copy.9
  234.0 75.2 %all-reduce.11.cloned.1.call-done = bf16[2,512,512]{2,1,0:T(8,128)(2,1)} async-done(((bf16[2,512,512]{2,1,0:T(8,128)(2,1)}), bf16[2,512,512]{2,1,0:T(8,128)(2,1)}) %all-reduce.11.cloned.1.call-update) | async-done | bytes 1048592 | tf_op jit(solution)/shard_map/psum | solution.py:29
  309.1 3.7 add_convert_fusion.7
  312.9 5.5 fusion.24
  318.4 1.9 copy.13
  320.3 3.1 fusion.15
  323.4 63.1 %reduce-scatter.3.cloned.1.call-done = bf16[2,64,512]{2,1,0:T(8,128)(2,1)} async-done(((bf16[2,512,512]{2,1,0:T(8,128)(2,1)}), bf16[2,64,512]{2,1,0:T(8,128)(2,1)}) %reduce-scatter.3.cloned.1.call-update) | async-done | bytes 131088 | tf_op jit(solution)/shard_map/reduce_scatter | solution.py:75
  386.5 1.6 fusion.26
  388.2 40.2 %all-gather.2.cloned.1.call-done = bf16[2,512,512]{2,1,0:T(8,128)(2,1)} async-done(((bf16[2,64,512]{2,1,0:T(8,128)(2,1)}), bf16[2,512,512]{2,1,0:T(8,128)(2,1)}) %all-gather.2.cloned.1.call-update) | async-done | bytes 1048592 | tf_op jit(solution)/shard_map/all_gather | solution.py:68
  428.4 4.0 fusion.11
  432.4 2.3 convolution_convert_fusion.2
  434.8 19.7 %psum.69 = f32[2]{0:T(128)S(1)} all-reduce(f32[2]{0:T(128)S(1)} %get-tuple-element.12), channel_id=1, replica_groups=mesh['layer'=4,'rows'=8] {'rows'}, use_global_device_ids=true, to_apply=%region_10.0 | all-reduce | flops 2 | bytes 16 | tf_op jit(solution)/shard_map/psum | solution.py:39
  454.4 57.5 %all-reduce.13.cloned.1.call-done = bf16[2,512,512]{2,1,0:T(8,128)(2,1)} async-done(((bf16[2,512,512]{2,1,0:T(8,128)(2,1)}), bf16[2,512,512]{2,1,0:T(8,128)(2,1)}) %all-reduce.13.cloned.1.call-update) | async-done | bytes 1048592 | tf_op jit(solution)/shard_map/psum | solution.py:29
  511.9 6.0 add_convert_fusion.6
  517.9 1.3 fusion.10
  519.2 1.3 copy-done.8
  520.6 2.3 convolution_convert_fusion.1
  522.9 77.8 %all-reduce.15.cloned.1.call-done = bf16[2,512,512]{2,1,0:T(8,128)(2,1)} async-done(((bf16[2,512,512]{2,1,0:T(8,128)(2,1)}), bf16[2,512,512]{2,1,0:T(8,128)(2,1)}) %all-reduce.15.cloned.1.call-update) | async-done | bytes 1048592 | tf_op jit(solution)/shard_map/psum | solution.py:29
  600.7 2.8 add_convert_fusion.5
  603.5 3.5 add_convert_fusion.1
  607.0 2.3 convolution_convert_fusion
  609.3 0.3 reduce-scatter.5.cloned.1.call-start
  609.6 77.5 %all-reduce.17.cloned.1.call-done = bf16[2,512,512]{2,1,0:T(8,128)(2,1)} async-done(((bf16[2,512,512]{2,1,0:T(8,128)(2,1)}), bf16[2,512,512]{2,1,0:T(8,128)(2,1)}) %all-reduce.17.cloned.1.call-update) | async-done | bytes 1048592 | tf_op jit(solution)/shard_map/psum | solution.py:29
  687.1 2.8 add_convert_fusion.4
  689.9 2.6 multiply_convert_fusion
  692.5 1.2 fusion.25
  693.8 1.8 copy.18
  695.6 3.1 fusion.13
  698.7 3.0 fusion.33
  701.8 60.1 %reduce-scatter.5.cloned.1.call-done = bf16[2,64,512]{2,1,0:T(8,128)(2,1)} async-done(((bf16[2,512,512]{2,1,0:T(8,128)(2,1)}), bf16[2,64,512]{2,1,0:T(8,128)(2,1)}) %reduce-scatter.5.cloned.1.call-update) | async-done | bytes 131088 | tf_op jit(solution)/shard_map/reduce_scatter | solution.py:75
  761.8 0.9 convert_add_fusion
  762.8 0.7 fusion.34
  (38 shorter events, 0.7 us)
Async XLA Ops:
  7.2 46.3 %copy-start = (bf16[1,1024,512]{2,1,0:T(8,128)(2,1)S(1)}, bf16[1,1024,512]{2,1,0:T(8,128)(2,1)}, u32[]{:S(2)}) copy-start(bf16[1,1024,512]{2,1,0:T(8,128)(2,1)} %param.7) | copy-start | bytes 3145732
  7.2 46.3 %copy-start.1 = (bf16[1,1024,512]{2,1,0:T(8,128)(2,1)S(1)}, bf16[1,1024,512]{2,1,0:T(8,128)(2,1)}, u32[]{:S(2)}) copy-start(bf16[1,1024,512]{2,1,0:T(8,128)(2,1)} %param.6) | copy-start | bytes 3145732
  7.2 127.1 %all-reduce.7.cloned.1.call-start = ((), (), s32[]{:S(2)}) async-start(), calls=%async_computation.2 | async-start | bytes 2097152 | tf_op jit(solution)/shard_map/psum | solution.py:29
  55.8 167.7 %all-reduce.9.cloned.1.call-start = ((), (), s32[]{:S(2)}) async-start(), calls=%async_computation.3 | async-start | bytes 2097152 | tf_op jit(solution)/shard_map/psum | solution.py:29
  142.0 1.3 copy-start.9
  145.6 80.8 %copy-start.10 = (bf16[2,1024,512]{2,1,0:T(8,128)(2,1)S(1)}, bf16[2,1024,512]{2,1,0:T(8,128)(2,1)}, u32[]{:S(2)}) copy-start(bf16[2,1024,512]{2,1,0:T(8,128)(2,1)} %copy-done.9) | copy-start | bytes 6291460
  145.6 163.5 %all-reduce.11.cloned.1.call-start = ((), (), s32[]{:S(2)}) async-start(), calls=%async_computation.4 | async-start | bytes 2097152 | tf_op jit(solution)/shard_map/psum | solution.py:29
  227.6 1.3 copy-start.7
  229.0 2.4 copy-start.2
  231.2 1.4 copy-start.3
  231.3 155.2 %reduce-scatter.3.cloned.1.call-start = ((), (), s32[]{:S(2)}) async-start(), calls=%async_computation.5 | async-start | bytes 1179648 | tf_op jit(solution)/shard_map/reduce_scatter | solution.py:75
  323.4 105.0 %all-gather.2.cloned.1.call-start = ((), (), s32[]{:S(2)}) async-start(), calls=%async_computation.6 | async-start | bytes 1179648 | tf_op jit(solution)/shard_map/all_gather | solution.py:68
  388.1 123.8 %all-reduce.13.cloned.1.call-start = ((), (), s32[]{:S(2)}) async-start(), calls=%async_computation.7 | async-start | bytes 2097152 | tf_op jit(solution)/shard_map/psum | solution.py:29
  434.7 166.0 %all-reduce.15.cloned.1.call-start = ((), (), s32[]{:S(2)}) async-start(), calls=%async_computation.8 | async-start | bytes 2097152 | tf_op jit(solution)/shard_map/psum | solution.py:29
  519.2 1.3 copy-start.8
  522.9 164.2 %all-reduce.17.cloned.1.call-start = ((), (), s32[]{:S(2)}) async-start(), calls=%async_computation.9 | async-start | bytes 2097152 | tf_op jit(solution)/shard_map/psum | solution.py:29
  609.3 152.6 %reduce-scatter.5.cloned.1.call-start = ((), (), s32[]{:S(2)}) async-start(), calls=%async_computation.10 | async-start | bytes 1179648 | tf_op jit(solution)/shard_map/reduce_scatter | solution.py:75
  689.9 2.7 copy-start.4
  689.9 2.7 copy-start.5
  698.7 63.1 %copy-start.6 = (bf16[2,64,512]{2,1,0:T(8,128)(2,1)S(1)}, bf16[2,64,512]{2,1,0:T(8,128)(2,1)}, u32[]{:S(2)}) copy-start(bf16[2,64,512]{2,1,0:T(8,128)(2,1)} %reduce-scatter.3.cloned.1.call-done) | copy-start | bytes 393220
Sparse Core Ops, SparseCore 0:
  55.9 78.3 all-reduce.6
  145.7 77.7 all-reduce.8
  231.4 77.6 all-reduce.10
  323.5 62.9 reduce-scatter.2
  389.1 39.2 all-gather.1
  434.8 77.0 all-reduce.12
  523.0 77.6 all-reduce.14
  609.4 77.6 all-reduce.16
  698.8 62.9 reduce-scatter.4
where the time goes:
time: 770 us
  waiting for transfers between devices  586 us (76%)
  blocking collectives  83.2 us (11%)
  matrix products  58.9 us (8%)
  between operations  14.7 us (2%)
  local copies, waits for them, and re-layouts  14.1 us (2%)
  other arithmetic  12.8 us (2%)
    psum x6, waiting for transfers between devices, polynomial(): lax.psum(partial_value.astype(jnp.bfloat16), 'rows').astype(jnp.float32)  422 us
    reduce_scatter x2, waiting for transfers between devices, on_device(): lax.psum_scatter(term.astype(jnp.bfloat16), 'rows', scatter_dimension=1,...  123 us
    psum x1, blocking collectives, on_device(): total = lax.psum(local_sum, ('layer', 'rows'))  42.2 us
    psum x2, blocking collectives, orthogonalize(): lax.psum(jnp.sum(jnp.square(shifted.astype(jnp.float32)), axis=(1, 2)), '...  41 us
    all_gather x1, waiting for transfers between devices, on_device(): shift = lax.all_gather(shift_rows, 'rows', axis=1, tiled=True)  40.2 us
    dot_general x6, matrix products, polynomial(): quartic = jnp.einsum('bcd,bde->bce', summed, summed, precision=highest)  24.2 us
    dot_general x8, matrix products, products(): jnp.einsum('brc,brd->bcd', left, right, preferred_element_type=jnp.float32)  20.4 us
  transfers between devices with their start and end apart: 9, of which 9 were waited for; matrix products, arithmetic and copies ran while one was open for 1% of the time, Pallas kernels for 0%

commit v1 on v0

v1 whole, which is shorter than its diff:
```python
import functools

import jax
import jax.numpy as jnp
from jax import lax
from jax.experimental import pallas as pl
from jax.experimental.pallas import tpu as pltpu
from jax.sharding import PartitionSpec as P

DUAL_ITERS = 2
NS_STEPS = 3
first_coeff = 3.4445
third_coeff = -4.775
fifth_coeff = 2.0315
learn_rate = 0.1
dual_rate = 4.0
clip_target = 0.02
epsilon = 1e-06

TILE = 128
F32 = jnp.float32
BF16 = jnp.bfloat16
VMEM = pl.BlockSpec(memory_space=pltpu.VMEM)


def block_list(nb):
    upper = [(i, j) for i in range(nb) for j in range(i, nb)]
    return (
        [("A", i, j) for i, j in upper]
        + [("D", i, j) for i, j in upper]
        + [("B", i, j) for i in range(nb) for j in range(nb)]
    )


def strips(nb):
    runs, place = [], 0
    for name in ("A", "D"):
        for i in range(nb):
            runs.append((name, i, i, place))
            place += nb - i
    for i in range(nb):
        runs.append(("B", i, 0, place))
        place += nb
    return runs


def gram_kernel(nb, kw, vw, kg, vg, own, other, tile, gt, wt):
    parity = lax.rem(lax.axis_index("rows"), 2)

    def one(w, g, dst):
        gt[...] = g[...].T
        wt[...] = w[...].T
        for name, i, j, place in strips(nb):
            left = wt if name in ("D", "B") else gt
            right = w if name == "D" else g
            rows = left[i * TILE : (i + 1) * TILE, :]
            value = jnp.dot(rows, right[:, j * TILE :], preferred_element_type=F32).astype(BF16)
            for step in range(nb - j):
                chunk, column = divmod(place + step, nb)
                dst[chunk, :, column * TILE : (column + 1) * TILE] = value[
                    :, step * TILE : (step + 1) * TILE
                ]

    total = jnp.zeros((8, g_cols(kg)), F32)
    rows = kg.shape[0]
    for ref in (kg, vg):
        for start in range(0, rows, 128):
            part = ref[start : start + 128, :].astype(F32)
            total = total + jnp.sum((part * part).reshape(16, 8, -1), axis=0)
    folded = total[:, :TILE]
    for i in range(1, nb):
        folded = folded + total[:, i * TILE : (i + 1) * TILE]
    tile[...] = folded

    @pl.when(parity == 0)
    def _():
        one(vw, vg, other)
        one(kw, kg, own)

    @pl.when(parity == 1)
    def _():
        one(kw, kg, other)
        one(vw, vg, own)


def g_cols(ref):
    return ref.shape[-1]


def reduce_kernel(
    layers, n, own, other, tile, out, total,
    acc, from_pair, from_left, from_right, to_left, to_right,
    layer_tiles, tile_sum, row_tiles,
    pair_sems, left_sems, right_sems, layer_sems, row_sems,
):
    layer = lax.axis_index("layer")
    r = lax.axis_index("rows")
    m = n // 2
    c = r // 2
    pair = r + 1 - 2 * lax.rem(r, 2)
    chunks = own.shape[0]
    MESH = pl.DeviceIdType.MESH

    barrier = pltpu.get_barrier_semaphore()
    for o in range(1, layers):
        peer = (lax.rem(layer + o, layers), r)
        pl.semaphore_signal(barrier, inc=1, device_id=peer, device_id_type=MESH)
    for o in range(1, n):
        peer = (layer, lax.rem(r + o, n))
        pl.semaphore_signal(barrier, inc=1, device_id=peer, device_id_type=MESH)
    pl.semaphore_wait(barrier, layers - 1 + n - 1)

    def layer_copy(o):
        return pltpu.make_async_remote_copy(
            src_ref=tile, dst_ref=layer_tiles.at[o - 1],
            send_sem=layer_sems.at[0, o - 1], recv_sem=layer_sems.at[1, o - 1],
            device_id=(lax.rem(layer + o, layers), r), device_id_type=MESH)

    def row_copy(o):
        return pltpu.make_async_remote_copy(
            src_ref=tile_sum, dst_ref=row_tiles.at[o - 1],
            send_sem=row_sems.at[0, o - 1], recv_sem=row_sems.at[1, o - 1],
            device_id=(layer, lax.rem(r + o, n)), device_id_type=MESH)

    def pair_copy(k):
        return pltpu.make_async_remote_copy(
            src_ref=other.at[k], dst_ref=from_pair.at[k],
            send_sem=pair_sems.at[0, k], recv_sem=pair_sems.at[1, k],
            device_id=(layer, pair), device_id_type=MESH)

    def right_copy(k):
        return pltpu.make_async_remote_copy(
            src_ref=to_right.at[k], dst_ref=from_left.at[k],
            send_sem=right_sems.at[0, k], recv_sem=right_sems.at[1, k],
            device_id=(layer, lax.rem(r + 2, n)), device_id_type=MESH)

    def left_copy(k):
        return pltpu.make_async_remote_copy(
            src_ref=to_left.at[k], dst_ref=from_right.at[k],
            send_sem=left_sems.at[0, k], recv_sem=left_sems.at[1, k],
            device_id=(layer, lax.rem(r + n - 2, n)), device_id_type=MESH)

    for o in range(1, layers):
        layer_copy(o).start()

    def begin(k, carry):
        pair_copy(k).start()
        return carry

    lax.fori_loop(0, chunks, begin, 0)
    for o in range(1, layers):
        layer_copy(o).wait_recv()
    value = tile[...]
    for o in range(1, layers):
        value = value + layer_tiles[o - 1]
    tile_sum[...] = value
    for o in range(1, n):
        row_copy(o).start()

    def step(t, carry):
        @pl.when(t < chunks)
        def _():
            pair_copy(t).wait_recv()
            both = own[t].astype(F32) + from_pair[t].astype(F32)
            acc[t] = both
            out[t] = both

        k = t - c

        @pl.when((k >= 0) & (k < chunks))
        def _():
            @pl.when(c > 0)
            def _():
                right_copy(k).wait_recv()
                out[k] = out[k] + from_left[k].astype(F32)

                @pl.when(c < m - 1)
                def _():
                    to_right[k] = (acc[k] + from_left[k].astype(F32)).astype(BF16)

            @pl.when(c == 0)
            def _():
                to_right[k] = acc[k].astype(BF16)

            @pl.when(c < m - 1)
            def _():
                right_copy(k).start()

        q = t - (m - 1 - c)

        @pl.when((q >= 0) & (q < chunks))
        def _():
            @pl.when(c < m - 1)
            def _():
                left_copy(q).wait_recv()
                out[q] = out[q] + from_right[q].astype(F32)

                @pl.when(c > 0)
                def _():
                    to_left[q] = (acc[q] + from_right[q].astype(F32)).astype(BF16)

            @pl.when(c == m - 1)
            def _():
                to_left[q] = acc[q].astype(BF16)

            @pl.when(c > 0)
            def _():
                left_copy(q).start()

        return carry

    lax.fori_loop(0, chunks + m - 1, step, 0)

    for o in range(1, n):
        row_copy(o).wait_recv()
    value = tile_sum[...]
    for o in range(1, n):
        value = value + row_tiles[o - 1]
    total[...] = value

    def end(k, carry):
        pair_copy(k).wait_send()

        @pl.when(c < m - 1)
        def _():
            right_copy(k).wait_send()

        @pl.when(c > 0)
        def _():
            left_copy(k).wait_send()

        return carry

    lax.fori_loop(0, chunks, end, 0)
    for o in range(1, layers):
        layer_copy(o).wait_send()
    for o in range(1, n):
        row_copy(o).wait_send()


def dual_kernel(nb, n, entries, packed, tile, send, dual, A, B, D, M, Q, T, L, S, F, U, h0, l0, h1, l1):
    size = nb * TILE
    half = size // 2
    r = lax.axis_index("rows")
    clip = clip_target * lax.rsqrt(jnp.full((1, TILE), jnp.sum(tile[...]) / entries + epsilon))
    clip = jnp.max(clip)

    for place, (name, i, j) in enumerate(block_list(nb)):
        chunk, column = divmod(place, nb)
        block = packed[chunk, :, column * TILE : (column + 1) * TILE]
        ref, scale = {"A": (A, clip * clip), "B": (B, clip), "D": (D, None)}[name]
        if scale is not None:
            block = block * scale
        ref[i * TILE : (i + 1) * TILE, j * TILE : (j + 1) * TILE] = block
        if name != "B" and i != j:
            ref[j * TILE : (j + 1) * TILE, i * TILE : (i + 1) * TILE] = block.T

    def split(ref, high, low):
        value = ref[...]
        rounded = value.astype(BF16)
        high[...] = rounded
        low[...] = (value - rounded.astype(F32)).astype(BF16)

    def split_dot(start, xh, xl, yh, yl):
        rows = pl.ds(start, half)
        return (
            jnp.dot(xh[rows, :], yh[...], preferred_element_type=F32)
            + jnp.dot(xh[rows, :], yl[...], preferred_element_type=F32)
            + jnp.dot(xl[rows, :], yh[...], preferred_element_type=F32)
        )

    def multiply(x, y, store):
        split(x, h0, l0)
        same = x is y
        if not same:
            split(y, h1, l1)

        def body(i, carry):
            start = pl.multiple_of(i * half, half)
            store(pl.ds(start, half), split_dot(start, h0, l0, h0 if same else h1, l0 if same else l1))
            return carry

        lax.fori_loop(0, 2, body, 0)

    def eye(rows_start):
        a = lax.broadcasted_iota(jnp.int32, (half, size), 0) + rows_start
        b = lax.broadcasted_iota(jnp.int32, (half, size), 1)
        return a == b

    def put(ref):
        def store(rows, value):
            ref[rows, :] = value
        return store

    def add(ref):
        def store(rows, value):
            ref[rows, :] = ref[rows, :] + value
        return store

    def orthogonalize():
        squares = jnp.float32(0)
        for i in range(2):
            squares = squares + jnp.sum(
                jnp.where(eye(i * half), M[i * half : (i + 1) * half, :], 0.0))
        whole = jnp.full((1, size), squares + epsilon)
        M[...] = M[...] * (1.0 / whole)
        inverse = lax.rsqrt(whole)
        for i in range(2):
            Q[i * half : (i + 1) * half, :] = jnp.where(eye(i * half), inverse, 0.0)

        def ns_step(k, carry):
            def poly(rows, value):
                T[rows, :] = third_coeff * M[rows, :] + fifth_coeff * value + jnp.where(
                    eye(rows.start), first_coeff, 0.0)
            multiply(M, M, poly)
            multiply(Q, T, put(U))
            Q[...] = U[...]

            @pl.when(k < NS_STEPS - 1)
            def _():
                multiply(M, T, put(U))
                multiply(T, U, put(M))
            return carry

        lax.fori_loop(0, NS_STEPS, ns_step, 0)

    def dual_step(first):
        multiply(B if first else F, Q, put(U))
        term = (dual_rate * -learn_rate) * (U[...] + U[...].T)
        L[...] = term if first else L[...] + term

    M[...] = A[...]
    orthogonalize()
    dual_step(True)
    for iteration in range(1, DUAL_ITERS):
        S[...] = 4.0 * L[...]
        F[...] = B[...]
        multiply(D, S, add(F))
        multiply(S, B, put(U))
        M[...] = A[...] + U[...].T
        multiply(S, F, add(M))
        orthogonalize()
        dual_step(False)
    send[0:size, :] = (Q[...] * (clip * -learn_rate)).astype(BF16)
    multiply(S, Q, put(U))
    send[size : 2 * size, :] = (U[...] * -learn_rate).astype(BF16)
    depth = size // n
    pair = r + 1 - 2 * lax.rem(r, 2)
    dual[...] = L[pl.ds(pl.multiple_of(r * depth, depth), depth), :]
    send[2 * size :, :] = L[pl.ds(pl.multiple_of(pair * depth, depth), depth), :].astype(BF16)


def on_device(key_weight, value_weight, key_grad, value_grad):
    layers, n = lax.axis_size("layer"), lax.axis_size("rows")
    kw, vw, kg, vg = (x.reshape(x.shape[1:]) for x in (key_weight, value_weight, key_grad, value_grad))
    rows, size = kw.shape
    nb = size // TILE
    chunks = 2 * nb + 1
    depth = size // n
    entries = 2.0 * rows * size * layers * n
    shape = jax.ShapeDtypeStruct
    packed = (chunks, TILE, size)
    limit = 48 * 1024 * 1024
    own, other, tile = pl.pallas_call(
        functools.partial(gram_kernel, nb),
        out_shape=(shape(packed, BF16), shape(packed, BF16), shape((8, TILE), F32)),
        in_specs=[VMEM] * 4,
        out_specs=(VMEM,) * 3,
        scratch_shapes=[pltpu.VMEM((size, rows), BF16)] * 2,
        compiler_params=pltpu.CompilerParams(vmem_limit_bytes=limit),
        name="grams",
    )(kw, vw, kg, vg)
    sums, total = pl.pallas_call(
        functools.partial(reduce_kernel, layers, n),
        out_shape=(shape(packed, F32), shape((8, TILE), F32)),
        in_specs=[VMEM] * 3,
        out_specs=(VMEM,) * 2,
        scratch_shapes=[pltpu.VMEM(packed, F32)]
        + [pltpu.VMEM(packed, BF16)] * 5
        + [
            pltpu.VMEM((layers - 1, 8, TILE), F32),
            pltpu.VMEM((8, TILE), F32),
            pltpu.VMEM((n - 1, 8, TILE), F32),
        ]
        + [pltpu.SemaphoreType.DMA((2, chunks))] * 3
        + [pltpu.SemaphoreType.DMA((2, layers - 1)), pltpu.SemaphoreType.DMA((2, n - 1))],
        compiler_params=pltpu.CompilerParams(
            collective_id=0, has_side_effects=True, vmem_limit_bytes=limit),
        name="reduce",
    )(own, other, tile)
    square = pltpu.VMEM((size, size), F32)
    send, dual = pl.pallas_call(
        functools.partial(dual_kernel, nb, n, entries),
        out_shape=(shape((2 * size + depth, size), BF16), shape((depth, size), F32)),
        in_specs=[VMEM] * 2,
        out_specs=(VMEM,) * 2,
        scratch_shapes=[square] * 10 + [pltpu.VMEM((size, size), BF16)] * 4,
        compiler_params=pltpu.CompilerParams(vmem_limit_bytes=limit),
        name="dual",
    )(sums, total)
    received = lax.ppermute(send, "rows", [(i, i + 1 - 2 * (i % 2)) for i in range(n)])
    even = lax.rem(lax.axis_index("rows"), 2) == 0
    received_dual = received[2 * size :].astype(F32)
    key_factor = jnp.where(even, send[: 2 * size], received[: 2 * size])
    value_factor = jnp.where(even, received[: 2 * size], send[: 2 * size])

    def update(g, w, factor):
        result = jnp.dot(g, factor[:size], preferred_element_type=F32)
        result = result + jnp.dot(w, factor[size:], preferred_element_type=F32)
        return result.astype(BF16)[None]

    return (
        update(kg, kw, key_factor),
        update(vg, vw, value_factor),
        jnp.where(even, dual, received_dual)[None],
        jnp.where(even, received_dual, dual)[None],
    )


def solution(mesh):
    placed = P("layer", "rows", None)
    return jax.shard_map(
        on_device,
        mesh=mesh,
        in_specs=(placed,) * 4,
        out_specs=(placed,) * 4,
        check_vma=False,
    )
```

time: 770 us -> 137 us (0.18)
  waiting for transfers between devices: 586 us -> 16.2 us
  Pallas kernels: 0 us -> 102 us
  blocking collectives: 83.2 us -> 0 us
  matrix products: 58.9 us -> 3.06 us
  between operations: 14.7 us -> 0.7 us
  other arithmetic: 12.8 us -> 1.71 us
    psum x6 -> x0, waiting for transfers between devices: 422 us -> none  [polynomial(): lax.psum(partial_value.astype(jnp.bfloat16), 'rows').astype(jnp.float32)]
    reduce_scatter x2 -> x0, waiting for transfers between devices: 123 us -> none  [on_device(): lax.psum_scatter(term.astype(jnp.bfloat16), 'rows', scatter_dimension=1,...]
    pallas_call x0 -> x3, Pallas kernels: none -> 102 us  [the longest x1 58.3 us: on_device(): pl.pallas_call(functools.partial(reduce_kernel, layers, n), out_shape=(sh...]
    psum x3 -> x0, blocking collectives: 83.2 us -> none  [the longest x1 42.2 us: on_device(): total = lax.psum(local_sum, ('layer', 'rows'))]
    dot_general x20 -> x4, matrix products: 58.9 us -> 3.06 us  [the longest x2 1.55 us: update(): result = jnp.dot(g, factor[:size], preferred_element_type=F32)]
    all_gather x1 -> x0, waiting for transfers between devices: 40.2 us -> none  [on_device(): shift = lax.all_gather(shift_rows, 'rows', axis=1, tiled=True)]
    ppermute x0 -> x1, waiting for transfers between devices: none -> 16.2 us  [on_device(): lax.ppermute(send, 'rows', [(i, i + 1 - 2 * (i % 2)) for i in range(n)])]
    convert_element_type x3 -> x0, other arithmetic: 7.79 us -> none  [the longest x2 6.21 us: on_device(): term.astype(jnp.bfloat16)]
  transfers between devices with their start and end apart: 9 -> 1, of which waited for: 9 -> 1; matrix products, arithmetic and copies ran while one was open for 1% -> 0% of each run, Pallas kernels for 0% -> 0%
where the time goes in v1:
time: 137 us; the launch traced here: 136 us
  Pallas kernels  102 us (74%)
  waiting for transfers between devices  16.2 us (12%)
  local copies, waits for them, and re-layouts  10.6 us (8%)
  matrix products  3.06 us (2%)
  starting transfers between devices  1.89 us (1%)
  other arithmetic  1.71 us (1%)
    pallas_call x1, Pallas kernels, on_device(): pl.pallas_call(functools.partial(reduce_kernel, layers, n), out_shape=(sh...  58.3 us
    pallas_call x1, Pallas kernels, on_device(): pl.pallas_call(functools.partial(dual_kernel, nb, n, entries), out_shape=...  39.6 us
    ppermute x1, waiting for transfers between devices, on_device(): lax.ppermute(send, 'rows', [(i, i + 1 - 2 * (i % 2)) for i in range(n)])  16.2 us
    unnamed x22, local copies, waits for them, and re-layouts  10.6 us
    pallas_call x1, Pallas kernels, on_device(): pl.pallas_call(functools.partial(gram_kernel, nb), out_shape=(shape(packe...  4.28 us
  transfers between devices with their start and end apart: 1, of which 1 were waited for; matrix products, arithmetic and copies ran while one was open for 0% of the time, Pallas kernels for 0%

profile of v1, /device:TPU:0, one launch (start us, length us, event | category | flops | bytes accessed | tf_op | source)
XLA Modules:
  0.0 136.2 jit_solution(2597608210146717225)
XLA Ops:
  0.6 0.0 copy-start
  0.6 1.2 copy-done
  1.9 0.0 copy-start.2
  1.9 1.2 copy-done.2
  3.1 0.0 copy-start.4
  3.1 1.2 copy-done.4
  4.3 0.0 copy-start.6
  4.3 1.2 copy-done.6
  5.5 4.3 %grams.1 = (bf16[9,128,512]{2,1,0:T(8,128)(2,1)S(1)}, bf16[9,128,512]{2,1,0:T(8,128)(2,1)}, f32[8,128]{1,0:T(8,128)S(1)}) custom-call(bf16[1024,512]{1,0:T(8,128)(2,1)S(1)} %bitcast.25, bf16[1024,512]{1,0:T(8,128)(2,1)S(1)} %bitcast.24, bf16[1024,512]{1,0:T(8,128)(2,1)S(1)} %bitcast.27, bf16[1024,512]{1,0:T(8,128)(2,1)S(1)} %bitcast.26), custom_call_target="tpu_custom_call" | custom-call | tf_op jit(solution)/shard_map/grams/pallas_call | solution.py:364
  9.8 0.0 copy-start.8
  9.8 1.3 copy-done.8
  11.1 58.3 %reduce.1 = (f32[9,128,512]{2,1,0:T(8,128)S(1)}, f32[8,128]{1,0:T(8,128)S(1)}) custom-call(bf16[9,128,512]{2,1,0:T(8,128)(2,1)S(1)} %get-tuple-element.11.own, bf16[9,128,512]{2,1,0:T(8,128)(2,1)S(1)} %copy-done.8, f32[8,128]{1,0:T(8,128)S(1)} %get-tuple-element.13.tile), custom_call_target="tpu_custom_call" | custom-call | tf_op jit(solution)/shard_map/reduce/pallas_call | solution.py:373
  69.4 39.6 %dual.1 = (bf16[1088,512]{1,0:T(8,128)(2,1)S(1)}, f32[64,512]{1,0:T(8,128)S(1)}) custom-call(f32[9,128,512]{2,1,0:T(8,128)S(1)} %get-tuple-element.14.packed, f32[8,128]{1,0:T(8,128)S(1)} %get-tuple-element.15.tile), custom_call_target="tpu_custom_call" | custom-call | tf_op jit(solution)/shard_map/dual/pallas_call | solution.py:392
  108.9 1.9 %collective-permute-start = (bf16[1088,512]{1,0:T(8,128)(2,1)S(1)}, bf16[1088,512]{1,0:T(8,128)(2,1)S(1)}, u32[]{:S(2)}, u32[]{:S(2)}) collective-permute-start(bf16[1088,512]{1,0:T(8,128)(2,1)S(1)} %get-tuple-element.16), channel_id=1, source_target_pairs={{0,1},{1,0},{2,3},{3,2},{4,5},{5,4},{6,7},{7,6},{8,9},{9,8},{10,11... | collective-permute-start | bytes 3342344 | tf_op jit(solution)/shard_map/ppermute | solution.py:401
  110.8 0.0 copy-start.1
  110.8 16.2 %collective-permute-done = bf16[1088,512]{1,0:T(8,128)(2,1)S(1)} collective-permute-done((bf16[1088,512]{1,0:T(8,128)(2,1)S(1)}, bf16[1088,512]{1,0:T(8,128)(2,1)S(1)}, u32[]{:S(2)}, u32[]{:S(2)}) %collective-permute-start) | collective-permute-done | bytes 1114144 | tf_op jit(solution)/shard_map/ppermute | solution.py:401
  127.0 0.0 copy-start.9
  127.0 0.1 broadcast_select_fusion
  127.2 0.9 copy-done.9
  128.0 0.0 copy-start.5
  128.0 0.0 copy-done.1
  128.0 0.8 fusion.2
  128.8 0.5 copy-done.5
  129.2 0.8 fusion.1
  130.0 0.0 copy-start.3
  130.0 1.3 copy.9
  131.3 0.0 copy-start.7
  131.3 0.0 copy-done.3
  131.4 0.8 fusion.5
  132.1 0.5 copy-done.7
  132.6 0.8 fusion
  133.4 1.3 copy.8
  134.7 1.6 %fusion.9 = (f32[1,64,512]{2,1,0:T(8,128)}, f32[1,64,512]{2,1,0:T(8,128)}) fusion(f32[64,512]{1,0:T(8,128)S(1)} %get-tuple-element.17, pred[]{:T(512)S(6)} %eq.3, bf16[1088,512]{1,0:T(8,128)(2,1)} %copy-done.9), kind=kLoop, calls=%fused_computation.15 | loop fusion | flops 98304 | bytes 458753 | tf_op jit(solution)/shard_map/broadcast_in_dim | solution.py:416
Async XLA Ops:
  0.6 1.2 copy-start
  1.9 1.2 copy-start.2
  3.1 1.2 copy-start.4
  4.3 1.2 copy-start.6
  9.8 1.3 copy-start.8
  108.9 18.1 %collective-permute-start = (bf16[1088,512]{1,0:T(8,128)(2,1)S(1)}, bf16[1088,512]{1,0:T(8,128)(2,1)S(1)}, u32[]{:S(2)}, u32[]{:S(2)}) collective-permute-start(bf16[1088,512]{1,0:T(8,128)(2,1)S(1)} %get-tuple-element.16), channel_id=1, source_target_pairs={{0,1},{1,0},{2,3},{3,2},{4,5},{5,4},{6,7},{7,6},{8,9},{9,8},{10,11... | collective-permute-start | bytes 3342344 | tf_op jit(solution)/shard_map/ppermute | solution.py:401
  110.8 17.2 %copy-start.1 = (bf16[1,1024,512]{2,1,0:T(8,128)(2,1)S(1)}, bf16[1,1024,512]{2,1,0:T(8,128)(2,1)}, u32[]{:S(2)}) copy-start(bf16[1,1024,512]{2,1,0:T(8,128)(2,1)} %param.5) | copy-start | bytes 3145732
  127.0 1.0 copy-start.9
  128.0 1.2 copy-start.5
  130.0 1.3 copy-start.3
  131.3 1.2 copy-start.7

commit v2 on v1

--- a/solution.py
+++ b/solution.py
@@ -18,6 +18,8 @@
 epsilon = 1e-06
 
 TILE = 128
+LAG = 2
+AHEAD = 3
 F32 = jnp.float32
 BF16 = jnp.bfloat16
 VMEM = pl.BlockSpec(memory_space=pltpu.VMEM)
@@ -88,8 +90,9 @@
 
 
 def reduce_kernel(
-    layers, n, own, other, tile, out, total,
+    layers, n, wide, own, other, tile, out, total,
     acc, from_pair, from_left, from_right, to_left, to_right,
+    wide_from_left, wide_from_right, wide_to_left, wide_to_right, passing,
     layer_tiles, tile_sum, row_tiles,
     pair_sems, left_sems, right_sems, layer_sems, row_sems,
 ):
@@ -128,17 +131,48 @@
             send_sem=pair_sems.at[0, k], recv_sem=pair_sems.at[1, k],
             device_id=(layer, pair), device_id_type=MESH)
 
-    def right_copy(k):
-        return pltpu.make_async_remote_copy(
-            src_ref=to_right.at[k], dst_ref=from_left.at[k],
-            send_sem=right_sems.at[0, k], recv_sem=right_sems.at[1, k],
-            device_id=(layer, lax.rem(r + 2, n)), device_id_type=MESH)
-
-    def left_copy(k):
-        return pltpu.make_async_remote_copy(
-            src_ref=to_left.at[k], dst_ref=from_right.at[k],
-            send_sem=left_sems.at[0, k], recv_sem=left_sems.at[1, k],
-            device_id=(layer, lax.rem(r + n - 2, n)), device_id_type=MESH)
+    def chain(src, dst, sems, offset):
+        def copy(k):
+            return pltpu.make_async_remote_copy(
+                src_ref=src.at[k], dst_ref=dst.at[k],
+                send_sem=sems.at[0, k], recv_sem=sems.at[1, k],
+                device_id=(layer, lax.rem(r + offset, n)), device_id_type=MESH)
+        return copy
+
+    rights = [
+        (wide_to_right, wide_from_left, chain(wide_to_right, wide_from_left, right_sems, 2)),
+        (to_right, from_left, chain(to_right, from_left, right_sems, 2)),
+    ]
+    lefts = [
+        (wide_to_left, wide_from_right, chain(wide_to_left, wide_from_right, left_sems, n - 2)),
+        (to_left, from_right, chain(to_left, from_right, left_sems, n - 2)),
+    ]
+
+    def hop(k, kinds, first, last):
+        for kind, (src, dst, copy) in enumerate(kinds):
+
+            @pl.when((k < wide) if kind == 0 else (k >= wide))
+            def _():
+                passing[...] = acc[k]
+
+                @pl.when(jnp.logical_not(first))
+                def _():
+                    copy(k).wait_recv()
+                    arrived = dst[k].astype(F32)
+                    out[k] = out[k] + arrived
+                    passing[...] = passing[...] + arrived
+
+                @pl.when(jnp.logical_not(last))
+                def _():
+                    src[k] = passing[...].astype(src.dtype)
+                    copy(k).start()
+
+    def hop_end(k, kinds, last):
+        for kind, (src, dst, copy) in enumerate(kinds):
+
+            @pl.when(((k < wide) if kind == 0 else (k >= wide)) & jnp.logical_not(last))
+            def _():
+                copy(k).wait_send()
 
     for o in range(1, layers):
         layer_copy(o).start()
@@ -147,7 +181,7 @@
         pair_copy(k).start()
         return carry
 
-    lax.fori_loop(0, chunks, begin, 0)
+    lax.fori_loop(0, AHEAD, begin, 0)
     for o in range(1, layers):
         layer_copy(o).wait_recv()
     value = tile[...]
@@ -158,6 +192,10 @@
         row_copy(o).start()
 
     def step(t, carry):
+        @pl.when(t + AHEAD < chunks)
+        def _():
+            pair_copy(t + AHEAD).start()
+
         @pl.when(t < chunks)
         def _():
             pair_copy(t).wait_recv()
@@ -165,51 +203,21 @@
             acc[t] = both
             out[t] = both
 
-        k = t - c
+        k = t - LAG * c
 
         @pl.when((k >= 0) & (k < chunks))
         def _():
-            @pl.when(c > 0)
-            def _():
-                right_copy(k).wait_recv()
-                out[k] = out[k] + from_left[k].astype(F32)
-
-                @pl.when(c < m - 1)
-                def _():
-                    to_right[k] = (acc[k] + from_left[k].astype(F32)).astype(BF16)
-
-            @pl.when(c == 0)
-            def _():
-                to_right[k] = acc[k].astype(BF16)
-
-            @pl.when(c < m - 1)
-            def _():
-                right_copy(k).start()
-
-        q = t - (m - 1 - c)
+            hop(k, rights, c == 0, c == m - 1)
+
+        q = t - LAG * (m - 1 - c)
 
         @pl.when((q >= 0) & (q < chunks))
         def _():
-            @pl.when(c < m - 1)
-            def _():
-                left_copy(q).wait_recv()
-                out[q] = out[q] + from_right[q].astype(F32)
-
-                @pl.when(c > 0)
-                def _():
-                    to_left[q] = (acc[q] + from_right[q].astype(F32)).astype(BF16)
-
-            @pl.when(c == m - 1)
-            def _():
-                to_left[q] = acc[q].astype(BF16)
-
-            @pl.when(c > 0)
-            def _():
-                left_copy(q).start()
+            hop(q, lefts, c == m - 1, c == 0)
 
         return carry
 
-    lax.fori_loop(0, chunks + m - 1, step, 0)
+    lax.fori_loop(0, chunks + LAG * (m - 1), step, 0)
 
     for o in range(1, n):
         row_copy(o).wait_recv()
@@ -220,15 +228,8 @@
 
     def end(k, carry):
         pair_copy(k).wait_send()
-
-        @pl.when(c < m - 1)
-        def _():
-            right_copy(k).wait_send()
-
-        @pl.when(c > 0)
-        def _():
-            left_copy(k).wait_send()
-
+        hop_end(k, rights, c == m - 1)
+        hop_end(k, lefts, c == 0)
         return carry
 
     lax.fori_loop(0, chunks, end, 0)
@@ -257,9 +258,10 @@
 
     def split(ref, high, low):
         value = ref[...]
-        rounded = value.astype(BF16)
-        high[...] = rounded
-        low[...] = (value - rounded.astype(F32)).astype(BF16)
+        scaled = value * 65537.0
+        leading = scaled - (scaled - value)
+        high[...] = leading.astype(BF16)
+        low[...] = (value - leading).astype(BF16)
 
     def split_dot(start, xh, xl, yh, yl):
         rows = pl.ds(start, half)
@@ -268,6 +270,19 @@
             + jnp.dot(xh[rows, :], yl[...], preferred_element_type=F32)
             + jnp.dot(xl[rows, :], yh[...], preferred_element_type=F32)
         )
+
+    def multiply_rounded(x, y, store):
+        h0[...] = x[...].astype(BF16)
+        same = x is y
+        if not same:
+            h1[...] = y[...].astype(BF16)
+
+        def body(i, carry):
+            rows = pl.ds(pl.multiple_of(i * half, half), half)
+            store(rows, jnp.dot(h0[rows, :], (h0 if same else h1)[...], preferred_element_type=F32))
+            return carry
+
+        lax.fori_loop(0, 2, body, 0)
 
     def multiply(x, y, store):
         split(x, h0, l0)
@@ -305,21 +320,31 @@
         whole = jnp.full((1, size), squares + epsilon)
         M[...] = M[...] * (1.0 / whole)
         inverse = lax.rsqrt(whole)
-        for i in range(2):
-            Q[i * half : (i + 1) * half, :] = jnp.where(eye(i * half), inverse, 0.0)
 
         def ns_step(k, carry):
             def poly(rows, value):
                 T[rows, :] = third_coeff * M[rows, :] + fifth_coeff * value + jnp.where(
                     eye(rows.start), first_coeff, 0.0)
-            multiply(M, M, poly)
-            multiply(Q, T, put(U))
-            Q[...] = U[...]
-
-            @pl.when(k < NS_STEPS - 1)
+            multiply_rounded(M, M, poly)
+
+            @pl.when(k == 0)
+            def _():
+                Q[...] = T[...] * inverse
+
+            @pl.when(k > 0)
+            def _():
+                multiply_rounded(Q, T, put(U))
+                Q[...] = U[...]
+
+            @pl.when(k == 0)
             def _():
                 multiply(M, T, put(U))
                 multiply(T, U, put(M))
+
+            @pl.when((k > 0) & (k < NS_STEPS - 1))
+            def _():
+                multiply_rounded(M, T, put(U))
+                multiply_rounded(T, U, put(M))
             return carry
 
         lax.fori_loop(0, NS_STEPS, ns_step, 0)
@@ -335,14 +360,14 @@
     for iteration in range(1, DUAL_ITERS):
         S[...] = 4.0 * L[...]
         F[...] = B[...]
-        multiply(D, S, add(F))
-        multiply(S, B, put(U))
+        multiply_rounded(D, S, add(F))
+        multiply_rounded(S, B, put(U))
         M[...] = A[...] + U[...].T
-        multiply(S, F, add(M))
+        multiply_rounded(S, F, add(M))
         orthogonalize()
         dual_step(False)
     send[0:size, :] = (Q[...] * (clip * -learn_rate)).astype(BF16)
-    multiply(S, Q, put(U))
+    multiply_rounded(S, Q, put(U))
     send[size : 2 * size, :] = (U[...] * -learn_rate).astype(BF16)
     depth = size // n
     pair = r + 1 - 2 * lax.rem(r, 2)
@@ -356,11 +381,12 @@
     rows, size = kw.shape
     nb = size // TILE
     chunks = 2 * nb + 1
+    wide = -(-(nb + 1) // 2)
     depth = size // n
     entries = 2.0 * rows * size * layers * n
     shape = jax.ShapeDtypeStruct
     packed = (chunks, TILE, size)
-    limit = 48 * 1024 * 1024
+    limit = 28 * 1024 * 1024
     own, other, tile = pl.pallas_call(
         functools.partial(gram_kernel, nb),
         out_shape=(shape(packed, BF16), shape(packed, BF16), shape((8, TILE), F32)),
@@ -371,12 +397,14 @@
         name="grams",
     )(kw, vw, kg, vg)
     sums, total = pl.pallas_call(
-        functools.partial(reduce_kernel, layers, n),
+        functools.partial(reduce_kernel, layers, n, wide),
         out_shape=(shape(packed, F32), shape((8, TILE), F32)),
         in_specs=[VMEM] * 3,
         out_specs=(VMEM,) * 2,
         scratch_shapes=[pltpu.VMEM(packed, F32)]
         + [pltpu.VMEM(packed, BF16)] * 5
+        + [pltpu.VMEM((wide,) + packed[1:], F32)] * 4
+        + [pltpu.VMEM(packed[1:], F32)]
         + [
             pltpu.VMEM((layers - 1, 8, TILE), F32),
             pltpu.VMEM((8, TILE), F32),

time: 137 us -> 128 us (0.934)
  Pallas kernels: 102 us -> 90.7 us
  waiting for transfers between devices: 16.2 us -> 21 us
    pallas_call x1, Pallas kernels: 39.6 us -> 24.4 us  [on_device(): pl.pallas_call(functools.partial(dual_kernel, nb, n, entries), out_shape=...]
    pallas_call x1, Pallas kernels: 58.3 us -> 63.1 us  [on_device(): pl.pallas_call(functools.partial(reduce_kernel, layers, n, wide), out_sha...]
    ppermute x1, waiting for transfers between devices: 16.2 us -> 21 us  [on_device(): lax.ppermute(send, 'rows', [(i, i + 1 - 2 * (i % 2)) for i in range(n)])]
    unnamed x22 -> x20, local copies, waits for them, and re-layouts: 10.6 us -> 9.33 us
where the time goes in v2:
time: 128 us; the launch traced here: 127 us
  Pallas kernels  90.7 us (71%)
  waiting for transfers between devices  21 us (16%)
  local copies, waits for them, and re-layouts  9.33 us (7%)
  matrix products  3.06 us (2%)
  other arithmetic  1.71 us (1%)
    pallas_call x1, Pallas kernels, on_device(): pl.pallas_call(functools.partial(reduce_kernel, layers, n, wide), out_sha...  63.1 us
    pallas_call x1, Pallas kernels, on_device(): pl.pallas_call(functools.partial(dual_kernel, nb, n, entries), out_shape=...  24.4 us
    ppermute x1, waiting for transfers between devices, on_device(): lax.ppermute(send, 'rows', [(i, i + 1 - 2 * (i % 2)) for i in range(n)])  21 us
    unnamed x20, local copies, waits for them, and re-layouts  9.33 us
    pallas_call x1, Pallas kernels, on_device(): pl.pallas_call(functools.partial(gram_kernel, nb), out_shape=(shape(packe...  3.25 us
  transfers between devices with their start and end apart: 1, of which 1 were waited for; matrix products, arithmetic and copies ran while one was open for 0% of the time, Pallas kernels for 0%

profile of v2, /device:TPU:0, one launch (start us, length us, event | category | flops | bytes accessed | tf_op | source)
XLA Modules:
  0.0 127.3 jit_solution(7146310893365074494)
XLA Ops:
  0.6 0.0 copy-start
  0.6 1.2 copy-done
  1.9 0.0 copy-start.2
  1.9 1.2 copy-done.2
  3.1 0.0 copy-start.4
  3.1 1.2 copy-done.4
  4.3 0.0 copy-start.6
  4.3 1.2 copy-done.6
  5.5 3.2 %grams.1 = (bf16[9,128,512]{2,1,0:T(8,128)(2,1)S(1)}, bf16[9,128,512]{2,1,0:T(8,128)(2,1)S(1)}, f32[8,128]{1,0:T(8,128)S(1)}) custom-call(bf16[1024,512]{1,0:T(8,128)(2,1)S(1)} %bitcast.25, bf16[1024,512]{1,0:T(8,128)(2,1)S(1)} %bitcast.24, bf16[1024,512]{1,0:T(8,128)(2,1)S(1)} %bitcast.27, bf16[1024,512]{1,0:T(8,128)(2,1)S(1)} %bitcast.26), custom_call_target="tpu_custom_call" | custom-call | tf_op jit(solution)/shard_map/grams/pallas_call | solution.py:390
  8.8 63.1 %reduce.1 = (f32[9,128,512]{2,1,0:T(8,128)S(1)}, f32[8,128]{1,0:T(8,128)S(1)}) custom-call(bf16[9,128,512]{2,1,0:T(8,128)(2,1)S(1)} %get-tuple-element.11.own, bf16[9,128,512]{2,1,0:T(8,128)(2,1)S(1)} %get-tuple-element.12.other, f32[8,128]{1,0:T(8,128)S(1)} %get-tuple-element.13.tile), custom_call_target="tpu_custom_call" | custom-call | tf_op jit(solution)/shard_map/reduce/pallas_call | solution.py:399
  71.9 24.4 %dual.1 = (bf16[1088,512]{1,0:T(8,128)(2,1)S(1)}, f32[64,512]{1,0:T(8,128)S(1)}) custom-call(f32[9,128,512]{2,1,0:T(8,128)S(1)} %get-tuple-element.14.packed, f32[8,128]{1,0:T(8,128)S(1)} %get-tuple-element.15.tile), custom_call_target="tpu_custom_call" | custom-call | tf_op jit(solution)/shard_map/dual/pallas_call | solution.py:420
  96.3 0.8 collective-permute-start
  97.1 0.0 copy-start.1
  97.1 21.0 %collective-permute-done = bf16[1088,512]{1,0:T(8,128)(2,1)S(1)} collective-permute-done((bf16[1088,512]{1,0:T(8,128)(2,1)S(1)}, bf16[1088,512]{1,0:T(8,128)(2,1)S(1)}, u32[]{:S(2)}, u32[]{:S(2)}) %collective-permute-start) | collective-permute-done | bytes 1114144 | tf_op jit(solution)/shard_map/ppermute | solution.py:429
  118.0 0.0 copy-start.8
  118.0 0.1 broadcast_select_fusion
  118.2 0.9 copy-done.8
  119.0 0.0 copy-start.5
  119.0 0.0 copy-done.1
  119.0 0.8 fusion.2
  119.8 0.5 copy-done.5
  120.3 0.8 fusion.1
  121.0 0.0 copy-start.3
  121.0 1.3 %copy.9 = bf16[1,1024,512]{2,1,0:T(8,128)(2,1)} copy(bf16[1,1024,512]{1,2,0:T(8,128)(2,1)S(1)} %fusion.1) | data formatting | bytes 2097152
  122.4 0.0 copy-start.7
  122.4 0.0 copy-done.3
  122.4 0.8 fusion.5
  123.1 0.5 copy-done.7
  123.6 0.8 fusion
  124.4 1.3 %copy.8 = bf16[1,1024,512]{2,1,0:T(8,128)(2,1)} copy(bf16[1,1024,512]{1,2,0:T(8,128)(2,1)S(1)} %fusion) | data formatting | bytes 2097152
  125.7 1.6 %fusion.9 = (f32[1,64,512]{2,1,0:T(8,128)}, f32[1,64,512]{2,1,0:T(8,128)}) fusion(f32[64,512]{1,0:T(8,128)S(1)} %get-tuple-element.17, pred[]{:T(512)S(6)} %eq.3, bf16[1088,512]{1,0:T(8,128)(2,1)} %copy-done.8), kind=kLoop, calls=%fused_computation.15 | loop fusion | flops 98304 | bytes 458753 | tf_op jit(solution)/shard_map/broadcast_in_dim | solution.py:444
Async XLA Ops:
  0.6 1.2 copy-start
  1.9 1.2 copy-start.2
  3.1 1.2 copy-start.4
  4.3 1.2 copy-start.6
  96.3 21.7 %collective-permute-start = (bf16[1088,512]{1,0:T(8,128)(2,1)S(1)}, bf16[1088,512]{1,0:T(8,128)(2,1)S(1)}, u32[]{:S(2)}, u32[]{:S(2)}) collective-permute-start(bf16[1088,512]{1,0:T(8,128)(2,1)S(1)} %get-tuple-element.16), channel_id=1, source_target_pairs={{0,1},{1,0},{2,3},{3,2},{4,5},{5,4},{6,7},{7,6},{8,9},{9,8},{10,11... | collective-permute-start | bytes 3342344 | tf_op jit(solution)/shard_map/ppermute | solution.py:429
  97.1 22.0 %copy-start.1 = (bf16[1,1024,512]{2,1,0:T(8,128)(2,1)S(1)}, bf16[1,1024,512]{2,1,0:T(8,128)(2,1)}, u32[]{:S(2)}) copy-start(bf16[1,1024,512]{2,1,0:T(8,128)(2,1)} %param.5) | copy-start | bytes 3145732
  118.0 1.0 copy-start.8
  119.0 1.2 copy-start.5
  121.0 1.3 %copy-start.3 = (bf16[1,1024,512]{2,1,0:T(8,128)(2,1)S(1)}, bf16[1,1024,512]{2,1,0:T(8,128)(2,1)}, u32[]{:S(2)}) copy-start(bf16[1,1024,512]{2,1,0:T(8,128)(2,1)} %param.4) | copy-start | bytes 3145732
  122.4 1.2 copy-start.7
